TPU v7x, 32 devices: a whole 2x2x4 slice. The times are simulated.
32 devices in a mesh: cluster: 4 (over x, core), blk: 8 (over z, y).
Axes of the slice: x: 2, y: 2, z: 4, core: 2. Of those that a mesh axis runs over, the one named last changes fastest.
Arguments:
- tokens: bfloat16 [6144, 2048], P(('cluster', 'blk')), may hold values from -40 to 40
- w_query: bfloat16 [2048, 2048], replicated, may hold values from -0.21875 to 0.21875
- w_key: bfloat16 [2048, 2048], replicated, may hold values from -0.21875 to 0.21875
- w_value: bfloat16 [2048, 2048], replicated, may hold values from -0.125 to 0.125
- cluster_ids: int32 [6144, 1], P(('cluster', 'blk')), may hold values from 0 to 3; in each aligned block of 192 rows (0 to 191, 192 to 383, ...) at most 64 rows name the same one
Outputs:
- attended: bfloat16 [6144, 2048], P(('cluster', 'blk'))
Inputs may be any that keep to these rules, and one draw needn't show every extreme that they name: `cluster_ids`: among the 192 tokens of one device no cluster appears more than 64 times; some device holds exactly 64 of some cluster; every cluster has tokens.
All inputs are finite; a program needn't handle non-finite values.
Results may differ from a plain program's by a relative error of at most 0.0045.
The roundings to bfloat16 on the way count: a program that leaves them out, or rounds other values in their place, can miss the bound.
Values may be sent and summed in bfloat16 or wider, within the bound.
A program may use at most 192 MiB of HBM per device.

v0:
```python
import jax
import jax.numpy as jnp
from jax import lax
from jax.sharding import PartitionSpec as P

HEADS = 16


MASKED_SCORE = -1e30


def project_rows(source, w_query, w_key, w_value):
    query = jnp.dot(source, w_query, preferred_element_type=jnp.float32).astype(jnp.bfloat16)
    keys_out = jnp.dot(source, w_key, preferred_element_type=jnp.float32).astype(jnp.bfloat16)
    values_out = jnp.dot(source, w_value, preferred_element_type=jnp.float32).astype(jnp.bfloat16)
    return (query, keys_out, values_out)


def per_device(tokens, w_query, w_key, w_value, cluster_ids):
    groups = lax.axis_size("cluster")
    tok_rows, model_width = tokens.shape
    head_count = HEADS
    head_size = model_width // head_count
    capacity = 4 * tok_rows // (3 * groups)
    slot_rows = capacity * groups
    score_scale = head_size ** (-0.5)
    labels = cluster_ids[:, 0]
    onehot = (labels[:, None] == jnp.arange(groups, dtype=jnp.int32)[None, :]).astype(jnp.int32)
    before = jnp.cumsum(onehot, axis=0) - onehot
    placed = jnp.sum(before * onehot, axis=1)
    counts = jnp.sum(onehot, axis=0)
    target = labels * capacity + placed
    live_send = (jnp.arange(capacity, dtype=jnp.int32)[None, :] < counts[:, None]).astype(
        jnp.bfloat16
    )
    query, keys_out, values_out = project_rows(tokens, w_query, w_key, w_value)
    packed = jnp.concatenate([query, keys_out, values_out], axis=1)
    outgoing = jnp.zeros((slot_rows, 3 * model_width), jnp.bfloat16).at[target].set(packed)
    arrived, live_in = (
        lax.all_to_all(
            outgoing.reshape(groups, capacity, 3 * model_width),
            "cluster",
            split_axis=0,
            concat_axis=0,
            tiled=True,
        ),
        lax.all_to_all(live_send, "cluster", split_axis=0, concat_axis=0, tiled=True),
    )
    arrived = arrived.reshape(slot_rows, 3 * model_width)
    q_rows = arrived[:, :model_width]
    k_rows = arrived[:, model_width : 2 * model_width]
    v_rows = arrived[:, 2 * model_width :]
    live_rows = live_in.reshape(slot_rows)
    query_heads = q_rows.reshape(slot_rows, head_count, head_size)
    initial = (
        jnp.full((head_count, slot_rows), MASKED_SCORE, jnp.float32),
        jnp.zeros((head_count, slot_rows), jnp.float32),
        jnp.zeros((slot_rows, head_count, head_size), jnp.float32),
    )
    running = initial
    key_piece = lax.all_gather(k_rows, "blk", axis=0, tiled=True)
    value_piece = lax.all_gather(v_rows, "blk", axis=0, tiled=True)
    live_piece = lax.all_gather(live_rows, "blk", axis=0, tiled=True)
    piece_rows = key_piece.shape[0]
    key_blocks = key_piece.reshape(piece_rows // slot_rows, slot_rows, head_count, head_size)
    value_blocks = value_piece.reshape(piece_rows // slot_rows, slot_rows, head_count, head_size)
    live_blocks = live_piece.reshape(piece_rows // slot_rows, slot_rows)

    def advance(state, operands):
        row_max, row_sum, numerator = state
        key_block, value_block, live_block = operands
        key_live = (live_block > 0)[None, None, :]
        scores = (
            jnp.einsum("qhd,khd->hqk", query_heads, key_block, preferred_element_type=jnp.float32)
            * score_scale
        )
        scores = jnp.where(key_live, scores, MASKED_SCORE)
        new_max = jnp.maximum(row_max, jnp.max(scores, axis=2))
        rescale = jnp.exp(row_max - new_max)
        softmax_w = jnp.where(key_live, jnp.exp(scores - new_max[:, :, None]), 0.0)
        row_sum = row_sum * rescale + jnp.sum(softmax_w, axis=2)
        numerator = numerator * jnp.transpose(rescale)[:, :, None] + jnp.einsum(
            "hqk,khd->qhd",
            softmax_w.astype(jnp.bfloat16),
            value_block,
            preferred_element_type=jnp.float32,
        )
        return ((new_max, row_sum, numerator), None)

    running, unused = lax.scan(advance, running, (key_blocks, value_blocks, live_blocks))
    row_max, row_sum, numerator = running
    attended = (
        (numerator / jnp.transpose(row_sum)[:, :, None])
        .astype(jnp.bfloat16)
        .reshape(slot_rows, model_width)
    )
    homeward = lax.all_to_all(
        attended.reshape(groups, capacity, model_width),
        "cluster",
        split_axis=0,
        concat_axis=0,
        tiled=True,
    )
    return homeward.reshape(slot_rows, model_width)[target]


def solution(mesh):
    return jax.shard_map(
        per_device,
        mesh=mesh,
        in_specs=(P(("cluster", "blk"), None), P(), P(), P(), P(("cluster", "blk"), None)),
        out_specs=P(("cluster", "blk"), None),
        check_vma=False,
    )
```

profile of v0, /device:TPU:0, one launch (start us, length us, event | category | flops | bytes accessed | tf_op | source)
XLA Modules:
  0.0 469.5 jit_solution(16651222645124500280)
XLA Ops:
  10.4 5.3 %convolution_convert_fusion = bf16[192,2048]{1,0:T(8,128)(2,1)S(1)} fusion(bf16[192,2048]{1,0:T(8,128)(2,1)S(1)} %copy-done, bf16[2048,2048]{1,0:T(8,128)(2,1)} %param.10), kind=kOutput, calls=%fused_computation.32 | convolution fusion | flops 1611005952 | bytes 9961472 | tf_op jit(solution)/shard_map/dot_general | solution.py:15
  20.8 5.9 %scatter_custom_fusion = bf16[256,6144]{1,0:T(8,128)(2,1)} fusion(s32[192]{0:T(256)S(1)} %bitcast.88, bf16[192,2048]{1,0:T(8,128)(2,1)S(1)} %convolution_convert_fusion, bf16[]{:T(256)} %constant.44, bf16[192,2048]{1,0:T(8,128)(2,1)S(1)} %convolution_convert_fusion.1, bf16[192,2048]{1,0:T(8,128)(2,1)S(1)} %convolution_convert_fusion.2, bf16[]{:T(256)} %constant.36.clone.1), kind=kCustom, calls=%fused_computation.35 | custom fusion | flops 7077888 | bytes 5505028 | tf_op jit(solution)/shard_map/scatter | solution.py:38
  26.6 41.2 %all_to_all.16 = bf16[4,64,6144]{2,1,0:T(8,128)(2,1)S(1)} all-to-all(bf16[4,64,6144]{2,1,0:T(8,128)(2,1)} %bitcast.78), channel_id=1, replica_groups=mesh['cluster'=4,'blk'=8] {'cluster'}, dimensions={0} | all-to-all | bytes 6291456 | tf_op jit(solution)/shard_map/all_to_all | solution.py:40
  70.9 3.2 all-to-all-start
  74.2 3.6 all-to-all-done
  77.9 21.9 %all-gather = bf16[8,1,256]{2,1,0:T(2,128)(2,1)S(1)} all-gather(bf16[1,1,256]{2,1,0:T(2,128)(2,1)S(1)} %reshape.106), channel_id=1, replica_groups=mesh['cluster'=4,'blk'=8] {'blk'}, dimensions={0}, use_global_device_ids=true | all-gather | bytes 4608 | tf_op jit(solution)/shard_map/all_gather | solution.py:63
  101.0 94.9 %all-gather.4.cloned.1.call-done = bf16[2048,2048]{1,0:T(8,128)(2,1)} async-done(((bf16[256,2048]{1,0:T(8,128)(2,1)}), bf16[2048,2048]{1,0:T(8,128)(2,1)}) %all-gather.4.cloned.1.call-update) | async-done | bytes 8388624 | tf_op jit(solution)/shard_map/all_gather | solution.py:61
  195.9 10.3 %copy.48 = bf16[256,8,16,128]{3,2,1,0:T(8,128)(2,1)} copy(bf16[256,8,16,128]{3,1,2,0:T(8,128)(2,1)} %bitcast.80) | data formatting | bytes 16777216
  206.2 115.0 %all-gather.6.cloned.1.call-done = bf16[2048,2048]{1,0:T(8,128)(2,1)} async-done(((bf16[256,2048]{1,0:T(8,128)(2,1)}), bf16[2048,2048]{1,0:T(8,128)(2,1)}) %all-gather.6.cloned.1.call-update) | async-done | bytes 8388624 | tf_op jit(solution)/shard_map/all_gather | solution.py:62
  321.2 9.7 %copy.49 = bf16[256,8,16,128]{3,2,1,0:T(8,128)(2,1)} copy(bf16[256,8,16,128]{3,1,2,0:T(8,128)(2,1)} %bitcast.81) | data formatting | bytes 16777216
  330.9 107.5 %while.15 = (s32[]{:T(128)}, f32[16,256]{1,0:T(8,128)S(1)}, f32[16,256]{1,0:T(8,128)S(1)}, f32[256,16,128]{0,2,1:T(8,128)}, bf16[8,256]{1,0:T(8,128)(2,1)S(1)}, ...) while((s32[]{:T(128)}, f32[16,256]{1,0:T(8,128)S(1)}, ...), condition=%wide.region_8.9_spmd.clone, body=%wide.region_5.8_spmd.clone.sunk | while | flops 552100608 | bytes 43255444 | solution.py:90
  332.9 2.8 bitcast_reduce_fusion.2
  337.3 5.4 %bitcast_add_fusion.2 = f32[256,16,128]{0,2,1:T(8,128)} fusion(f32[256,16,128]{0,2,1:T(8,128)} %get-tuple-element.210, f32[16,256,256]{2,1,0:T(8,128)} %get-tuple-element.194, f32[16,256]{1,0:T(8,128)S(1)} %get-tuple-element.218, pred[256]{0:T(512)(128)(4,1)S(1)} %compare_reduce_fusion.2, bf16[1,256,16,128]{1,3,2,0:T(8,128)(2,1)} %copy.61, ...), kind=kOutput, calls=%fused_computation.10.clone.1 | convolution fusion | flops 275251200 | bytes 9470209 | tf_op jit(solution)/shard_map/while/body/eval_jaxpr/hqk,khd->qhd/dot_general | solution.py:82
  345.8 2.8 bitcast_reduce_fusion.2
  350.2 6.0 %bitcast_add_fusion.2 = f32[256,16,128]{0,2,1:T(8,128)} fusion(f32[256,16,128]{0,2,1:T(8,128)} %get-tuple-element.210, f32[16,256,256]{2,1,0:T(8,128)} %get-tuple-element.194, f32[16,256]{1,0:T(8,128)S(1)} %get-tuple-element.218, pred[256]{0:T(512)(128)(4,1)S(1)} %compare_reduce_fusion.2, bf16[1,256,16,128]{1,3,2,0:T(8,128)(2,1)} %copy.61, ...), kind=kOutput, calls=%fused_computation.10.clone.1 | convolution fusion | flops 275251200 | bytes 9470209 | tf_op jit(solution)/shard_map/while/body/eval_jaxpr/hqk,khd->qhd/dot_general | solution.py:82
  359.3 2.8 bitcast_reduce_fusion.2
  363.7 6.0 %bitcast_add_fusion.2 = f32[256,16,128]{0,2,1:T(8,128)} fusion(f32[256,16,128]{0,2,1:T(8,128)} %get-tuple-element.210, f32[16,256,256]{2,1,0:T(8,128)} %get-tuple-element.194, f32[16,256]{1,0:T(8,128)S(1)} %get-tuple-element.218, pred[256]{0:T(512)(128)(4,1)S(1)} %compare_reduce_fusion.2, bf16[1,256,16,128]{1,3,2,0:T(8,128)(2,1)} %copy.61, ...), kind=kOutput, calls=%fused_computation.10.clone.1 | convolution fusion | flops 275251200 | bytes 9470209 | tf_op jit(solution)/shard_map/while/body/eval_jaxpr/hqk,khd->qhd/dot_general | solution.py:82
  370.9 1.9 constant_dynamic-slice_fusion.3
  372.8 2.8 bitcast_reduce_fusion.2
  377.2 6.0 %bitcast_add_fusion.2 = f32[256,16,128]{0,2,1:T(8,128)} fusion(f32[256,16,128]{0,2,1:T(8,128)} %get-tuple-element.210, f32[16,256,256]{2,1,0:T(8,128)} %get-tuple-element.194, f32[16,256]{1,0:T(8,128)S(1)} %get-tuple-element.218, pred[256]{0:T(512)(128)(4,1)S(1)} %compare_reduce_fusion.2, bf16[1,256,16,128]{1,3,2,0:T(8,128)(2,1)} %copy.61, ...), kind=kOutput, calls=%fused_computation.10.clone.1 | convolution fusion | flops 275251200 | bytes 9470209 | tf_op jit(solution)/shard_map/while/body/eval_jaxpr/hqk,khd->qhd/dot_general | solution.py:82
  386.3 2.8 bitcast_reduce_fusion.2
  390.7 6.0 %bitcast_add_fusion.2 = f32[256,16,128]{0,2,1:T(8,128)} fusion(f32[256,16,128]{0,2,1:T(8,128)} %get-tuple-element.210, f32[16,256,256]{2,1,0:T(8,128)} %get-tuple-element.194, f32[16,256]{1,0:T(8,128)S(1)} %get-tuple-element.218, pred[256]{0:T(512)(128)(4,1)S(1)} %compare_reduce_fusion.2, bf16[1,256,16,128]{1,3,2,0:T(8,128)(2,1)} %copy.61, ...), kind=kOutput, calls=%fused_computation.10.clone.1 | convolution fusion | flops 275251200 | bytes 9470209 | tf_op jit(solution)/shard_map/while/body/eval_jaxpr/hqk,khd->qhd/dot_general | solution.py:82
  397.9 1.9 constant_dynamic-slice_fusion.3
  399.8 2.8 bitcast_reduce_fusion.2
  404.2 6.0 %bitcast_add_fusion.2 = f32[256,16,128]{0,2,1:T(8,128)} fusion(f32[256,16,128]{0,2,1:T(8,128)} %get-tuple-element.210, f32[16,256,256]{2,1,0:T(8,128)} %get-tuple-element.194, f32[16,256]{1,0:T(8,128)S(1)} %get-tuple-element.218, pred[256]{0:T(512)(128)(4,1)S(1)} %compare_reduce_fusion.2, bf16[1,256,16,128]{1,3,2,0:T(8,128)(2,1)} %copy.61, ...), kind=kOutput, calls=%fused_computation.10.clone.1 | convolution fusion | flops 275251200 | bytes 9470209 | tf_op jit(solution)/shard_map/while/body/eval_jaxpr/hqk,khd->qhd/dot_general | solution.py:82
  413.4 2.8 bitcast_reduce_fusion.2
  417.8 6.0 %bitcast_add_fusion.2 = f32[256,16,128]{0,2,1:T(8,128)} fusion(f32[256,16,128]{0,2,1:T(8,128)} %get-tuple-element.210, f32[16,256,256]{2,1,0:T(8,128)} %get-tuple-element.194, f32[16,256]{1,0:T(8,128)S(1)} %get-tuple-element.218, pred[256]{0:T(512)(128)(4,1)S(1)} %compare_reduce_fusion.2, bf16[1,256,16,128]{1,3,2,0:T(8,128)(2,1)} %copy.61, ...), kind=kOutput, calls=%fused_computation.10.clone.1 | convolution fusion | flops 275251200 | bytes 9470209 | tf_op jit(solution)/shard_map/while/body/eval_jaxpr/hqk,khd->qhd/dot_general | solution.py:82
  426.9 2.8 bitcast_reduce_fusion.2
  431.3 6.0 %bitcast_add_fusion.2 = f32[256,16,128]{0,2,1:T(8,128)} fusion(f32[256,16,128]{0,2,1:T(8,128)} %get-tuple-element.210, f32[16,256,256]{2,1,0:T(8,128)} %get-tuple-element.194, f32[16,256]{1,0:T(8,128)S(1)} %get-tuple-element.218, pred[256]{0:T(512)(128)(4,1)S(1)} %compare_reduce_fusion.2, bf16[1,256,16,128]{1,3,2,0:T(8,128)(2,1)} %copy.61, ...), kind=kOutput, calls=%fused_computation.10.clone.1 | convolution fusion | flops 275251200 | bytes 9470209 | tf_op jit(solution)/shard_map/while/body/eval_jaxpr/hqk,khd->qhd/dot_general | solution.py:82
  442.7 3.5 all-to-all-start.2
  446.2 14.4 %all-to-all-done.2 = bf16[4,64,2048]{2,1,0:T(8,128)(2,1)S(1)} async-done(((bf16[4,64,2048]{2,1,0:T(8,128)(2,1)}), bf16[4,64,2048]{2,1,0:T(8,128)(2,1)S(1)}, u32[]{:S(2)}, u32[]{:S(2)}) %all-to-all-start.2) | async-done | bytes 1048608 | tf_op jit(solution)/shard_map/all_to_all | solution.py:97
  460.6 2.0 gather_fusion
  (114 shorter events, 50.9 us)
Async XLA Ops:
  6.5 3.9 copy-start
  6.5 189.4 %all-gather.4.cloned.1.call-start = ((), (), s32[]{:S(2)}) async-start(), calls=%async_computation.3 | async-start | bytes 9437184 | tf_op jit(solution)/shard_map/all_gather | solution.py:61
  10.4 5.8 %copy-start.3 = (bf16[2048,2048]{1,0:T(8,128)(2,1)S(1)}, bf16[2048,2048]{1,0:T(8,128)(2,1)}, u32[]{:S(2)}) copy-start(bf16[2048,2048]{1,0:T(8,128)(2,1)} %param.9) | copy-start | bytes 25165828
  10.4 7.7 %slice-start = ((s8[8388608]{0:T(1024)(128)(4,1)}), s8[4194304]{0:T(1024)(128)(4,1)S(1)}, s32[]{:S(2)}) async-start(s8[8388608]{0:T(1024)(128)(4,1)} %bitcast.92), calls=%async_computation.5 | async-start | bytes 8388608
  16.2 2.6 slice-start.1
  69.5 251.7 %all-gather.6.cloned.1.call-start = ((), (), s32[]{:S(2)}) async-start(), calls=%async_computation.4 | async-start | bytes 9437184 | tf_op jit(solution)/shard_map/all_gather | solution.py:62
  70.9 6.9 %all-to-all-start = ((bf16[4,1,64]{2,1,0:T(2,128)(2,1)}), bf16[4,1,64]{2,1,0:T(2,128)(2,1)S(1)}, u32[]{:S(2)}, u32[]{:S(2)}) async-start(bf16[4,1,64]{2,1,0:T(2,128)(2,1)} %compare_convert_fusion), calls=%async_computation | async-start | bytes 4096 | tf_op jit(solution)/shard_map/all_to_all | solution.py:47
  337.3 5.4 %copy-start.2 = (f32[16,256,256]{2,1,0:T(8,128)S(1)}, f32[16,256,256]{2,1,0:T(8,128)}, u32[]{:S(2)}) copy-start(f32[16,256,256]{2,1,0:T(8,128)} %get-tuple-element.194) | copy-start | bytes 12582916 | tf_op jit(solution)/shard_map/while
  350.1 6.0 %copy-start.2 = (f32[16,256,256]{2,1,0:T(8,128)S(1)}, f32[16,256,256]{2,1,0:T(8,128)}, u32[]{:S(2)}) copy-start(f32[16,256,256]{2,1,0:T(8,128)} %get-tuple-element.194) | copy-start | bytes 12582916 | tf_op jit(solution)/shard_map/while
  363.7 6.0 %copy-start.2 = (f32[16,256,256]{2,1,0:T(8,128)S(1)}, f32[16,256,256]{2,1,0:T(8,128)}, u32[]{:S(2)}) copy-start(f32[16,256,256]{2,1,0:T(8,128)} %get-tuple-element.194) | copy-start | bytes 12582916 | tf_op jit(solution)/shard_map/while
  377.2 6.0 %copy-start.2 = (f32[16,256,256]{2,1,0:T(8,128)S(1)}, f32[16,256,256]{2,1,0:T(8,128)}, u32[]{:S(2)}) copy-start(f32[16,256,256]{2,1,0:T(8,128)} %get-tuple-element.194) | copy-start | bytes 12582916 | tf_op jit(solution)/shard_map/while
  390.7 6.0 %copy-start.2 = (f32[16,256,256]{2,1,0:T(8,128)S(1)}, f32[16,256,256]{2,1,0:T(8,128)}, u32[]{:S(2)}) copy-start(f32[16,256,256]{2,1,0:T(8,128)} %get-tuple-element.194) | copy-start | bytes 12582916 | tf_op jit(solution)/shard_map/while
  404.2 6.0 %copy-start.2 = (f32[16,256,256]{2,1,0:T(8,128)S(1)}, f32[16,256,256]{2,1,0:T(8,128)}, u32[]{:S(2)}) copy-start(f32[16,256,256]{2,1,0:T(8,128)} %get-tuple-element.194) | copy-start | bytes 12582916 | tf_op jit(solution)/shard_map/while
  417.8 6.0 %copy-start.2 = (f32[16,256,256]{2,1,0:T(8,128)S(1)}, f32[16,256,256]{2,1,0:T(8,128)}, u32[]{:S(2)}) copy-start(f32[16,256,256]{2,1,0:T(8,128)} %get-tuple-element.194) | copy-start | bytes 12582916 | tf_op jit(solution)/shard_map/while
  431.3 6.0 %copy-start.2 = (f32[16,256,256]{2,1,0:T(8,128)S(1)}, f32[16,256,256]{2,1,0:T(8,128)}, u32[]{:S(2)}) copy-start(f32[16,256,256]{2,1,0:T(8,128)} %get-tuple-element.194) | copy-start | bytes 12582916 | tf_op jit(solution)/shard_map/while
  441.4 21.3 %copy-start.1 = (bf16[192,2048]{1,0:T(8,128)(2,1)S(1)}, bf16[192,2048]{1,0:T(8,128)(2,1)}, u32[]{:S(2)}) copy-start(bf16[192,2048]{1,0:T(8,128)(2,1)} %param.7) | copy-start | bytes 2359300
  442.7 18.0 %all-to-all-start.2 = ((bf16[4,64,2048]{2,1,0:T(8,128)(2,1)}), bf16[4,64,2048]{2,1,0:T(8,128)(2,1)S(1)}, u32[]{:S(2)}, u32[]{:S(2)}) async-start(bf16[4,64,2048]{2,1,0:T(8,128)(2,1)} %reshape_reshape.3), calls=%async_computation.2 | async-start | bytes 2097152 | tf_op jit(solution)/shard_map/all_to_all | solution.py:97
Sparse Core Ops, SparseCore 0:
  69.6 126.2 all-gather.3
  198.0 123.1 all-gather.5
where the time goes:
time: 470 us; the launch traced here: 469 us
  waiting for transfers between devices  229 us (49%)
  matrix products  79 us (17%)
  blocking collectives  63.2 us (13%)
  local copies, waits for them, and re-layouts  56.9 us (12%)
  other arithmetic  21.2 us (5%)
  between operations  13.5 us (3%)
  starting transfers between devices  6.78 us (1%)
    all_gather x1, waiting for transfers between devices, per_device(): value_piece = lax.all_gather(v_rows, 'blk', axis=0, tiled=True)  115 us
    all_gather x1, waiting for transfers between devices, per_device(): key_piece = lax.all_gather(k_rows, 'blk', axis=0, tiled=True)  94.9 us
    dot_general x8, matrix products, advance(): jnp.einsum('hqk,khd->qhd', softmax_w.astype(jnp.bfloat16), value_block, p...  47.5 us
    all_to_all x1, blocking collectives, per_device(): lax.all_to_all(outgoing.reshape(groups, capacity, 3 * model_width), 'clus...  41.2 us
    dynamic_slice x16, local copies, waits for them, and re-layouts, per_device(): lax.scan(advance, running, (key_blocks, value_blocks, live_blocks))  28 us
    dot_general x8, matrix products, advance(): jnp.einsum('qhd,khd->hqk', query_heads, key_block, preferred_element_type...  22.3 us
    unnamed x16, local copies, waits for them, and re-layouts  22 us
    all_gather x1, blocking collectives, per_device(): live_piece = lax.all_gather(live_rows, 'blk', axis=0, tiled=True)  21.9 us
  transfers between devices with their start and end apart: 4, of which 4 were waited for; matrix products, arithmetic and copies ran while one was open for 3% of the time, Pallas kernels for 0%

commit v1 on v0

v1 whole, which is shorter than its diff:
```python
import functools

import jax
import jax.numpy as jnp
from jax import lax
from jax.experimental import pallas as pl
from jax.experimental.pallas import tpu as pltpu
from jax.sharding import PartitionSpec as P

HEADS = 16
MASKED_SCORE = -1e30
LOG2E = 1.4426950408889634
PAIR = 2
GROUP = 4
MESH = pl.DeviceIdType.MESH


def kernel(groups, blks, parts, cap, tok_ref, wq_ref, wk_ref, wv_ref, lrow_ref, lcol_ref, out_ref,
           w_buf, kv_out, q_out, ids_out, kv_all, q_in, ids_all, k_slots, v_slots, q_slots, att_slots,
           ret_out, gathered, w_sem, kv_ss, kv_rs, q_ss, q_rs, id_ss, id_rs, fkv_ss, fkv_rs, fid_ss,
           fid_rs, ret_ss, ret_rs, own_sem):
    rows, width = tok_ref.shape
    size = width // HEADS
    slots = groups * cap
    pairs = HEADS // PAIR
    pw = PAIR * size
    ci, bi = lax.axis_index("cluster"), lax.axis_index("blk")
    part = lax.rem(ci, parts)
    me = (ci // parts) * blks + bi
    own_pair = me // PAIR

    def holder(head, its_part):
        return {"cluster": (head // blks) * parts + its_part, "blk": lax.rem(head, blks)}

    def pair_out(t):
        return lax.rem(own_pair + t, pairs)

    def source_at(i):
        return lax.rem(own_pair + pairs - i // PAIR, pairs) * PAIR + lax.rem(i, PAIR)

    def w_copies(t, slot):
        cols = pl.ds(pl.multiple_of(pair_out(t) * pw, pw), pw)
        return [
            pltpu.make_async_copy(ref.at[:, cols], w_buf.at[slot, :, pl.ds(n * pw, pw)], w_sem.at[slot, n])
            for n, ref in enumerate((wq_ref, wk_ref, wv_ref))
        ]

    for copy in w_copies(0, 0):
        copy.start()

    barrier = pltpu.get_barrier_semaphore()

    @pl.loop(0, HEADS)
    def _(h):
        @pl.when(h != me)
        def _():
            pl.semaphore_signal(barrier, inc=1, device_id=holder(h, part), device_id_type=MESH)

    for d in range(1, parts):
        pl.semaphore_signal(
            barrier, inc=1, device_id=holder(me, lax.rem(part + d, parts)), device_id_type=MESH
        )

    lab = lrow_ref[...]
    padded = lab.shape[1]
    earlier = (lcol_ref[...] == lab) & (
        lax.broadcasted_iota(jnp.int32, (rows, padded), 0)
        < lax.broadcasted_iota(jnp.int32, (rows, padded), 1)
    )
    rank = jnp.sum(earlier.astype(jnp.int32), axis=0, keepdims=True)
    target = jnp.where(lab >= 0, lab * cap + rank, -1)
    ids_out[...] = target
    ids_all[part, me] = target
    unit = (lax.broadcasted_iota(jnp.int32, (GROUP * cap, size), 1) == 0).astype(jnp.bfloat16)
    for c in range(groups):
        q_slots[c, :, size:] = unit

    pl.semaphore_wait(barrier, HEADS - 1 + parts - 1)

    def id_copy(h):
        return pltpu.make_async_remote_copy(
            ids_out, ids_all.at[part, me], id_ss.at[h], id_rs.at[me],
            device_id=holder(h, part), device_id_type=MESH)

    def kv_copy(h):
        return pltpu.make_async_remote_copy(
            kv_out.at[h], kv_all.at[part, me], kv_ss.at[h], kv_rs.at[me],
            device_id=holder(h, part), device_id_type=MESH)

    def q_copy(h):
        return pltpu.make_async_remote_copy(
            q_out.at[h], q_in.at[me], q_ss.at[h], q_rs.at[me],
            device_id=holder(h, part), device_id_type=MESH)

    def ret_copy(s):
        return pltpu.make_async_remote_copy(
            ret_out.at[s], gathered.at[:, pl.ds(pl.multiple_of(me * size, size), size)],
            ret_ss.at[s], ret_rs.at[me], device_id=holder(s, part), device_id_type=MESH)

    def kv_fwd(s, d):
        return pltpu.make_async_remote_copy(
            kv_all.at[part, s], kv_all.at[part, s], fkv_ss.at[d - 1, s], fkv_rs.at[d - 1, s],
            device_id=holder(me, lax.rem(part + d, parts)), device_id_type=MESH)

    def id_fwd(s, d):
        return pltpu.make_async_remote_copy(
            ids_all.at[part, s], ids_all.at[part, s], fid_ss.at[d - 1, s], fid_rs.at[d - 1, s],
            device_id=holder(me, lax.rem(part + d, parts)), device_id_type=MESH)

    @pl.loop(0, HEADS)
    def _(h):
        @pl.when(h != me)
        def _():
            id_copy(h).start()

    @pl.loop(0, pairs)
    def _(t):
        slot = lax.rem(t, 2)

        @pl.when(t + 1 < pairs)
        def _():
            for copy in w_copies(t + 1, 1 - slot):
                copy.start()

        for copy in w_copies(t, slot):
            copy.wait()
        made = jnp.dot(tok_ref[...], w_buf[slot], preferred_element_type=jnp.float32).astype(jnp.bfloat16)
        for j in range(PAIR):
            h = pair_out(t) * PAIR + j
            q = made[:, j * size:(j + 1) * size]
            k = made[:, pw + j * size:pw + (j + 1) * size]
            v = made[:, 2 * pw + j * size:2 * pw + (j + 1) * size]

            @pl.when(h != me)
            def _():
                kv_out[h, :, :size] = k
                kv_out[h, :, size:] = v
                q_out[h] = q
                kv_copy(h).start()

            @pl.when(h == me)
            def _():
                kv_all[part, me, :, :size] = k
                kv_all[part, me, :, size:] = v
                q_in[me] = q

    @pl.loop(0, HEADS)
    def _(i):
        h = lax.rem(own_pair * PAIR + i, HEADS)

        @pl.when(h != me)
        def _():
            q_copy(h).start()

    def spread(its_part, s):
        where = ids_all[its_part, s][:, :rows]
        return lax.broadcasted_iota(jnp.int32, (slots, rows), 0) == where

    def place_kv(its_part, s):
        hot = spread(its_part, s)
        placed = jnp.dot(
            hot.astype(jnp.bfloat16), kv_all[its_part, s], preferred_element_type=jnp.float32
        ).astype(jnp.bfloat16)
        live = jnp.sum(hot.astype(jnp.float32), axis=1, keepdims=True)
        bias = jnp.broadcast_to(jnp.where(live > 0, 0.0, MASKED_SCORE), (slots, size)).astype(jnp.bfloat16)
        at = pl.ds(pl.multiple_of((its_part * HEADS + s) * cap, cap), cap)
        for c in range(groups):
            mine = slice(c * cap, (c + 1) * cap)
            k_slots[c, at, :size] = placed[mine, :size]
            k_slots[c, at, size:] = bias[mine]
            v_slots[c, at, :] = placed[mine, size:]

    @pl.loop(0, HEADS)
    def _(i):
        s = source_at(i)

        @pl.when(s != me)
        def _():
            pltpu.make_async_remote_copy(
                ids_out, ids_all.at[part, s], id_ss.at[s], id_rs.at[s],
                device_id=holder(s, part), device_id_type=MESH).wait_recv()
            pltpu.make_async_remote_copy(
                kv_out.at[s], kv_all.at[part, s], kv_ss.at[s], kv_rs.at[s],
                device_id=holder(s, part), device_id_type=MESH).wait_recv()

        for d in range(1, parts):
            id_fwd(s, d).start()
            kv_fwd(s, d).start()
        place_kv(part, s)

    for d in range(1, parts):
        frm = lax.rem(part + parts - d, parts)

        @pl.loop(0, HEADS)
        def _(i):
            s = source_at(i)
            pltpu.make_async_remote_copy(
                ids_all.at[frm, s], ids_all.at[frm, s], fid_ss.at[d - 1, s], fid_rs.at[d - 1, s],
                device_id=holder(me, frm), device_id_type=MESH).wait_recv()
            pltpu.make_async_remote_copy(
                kv_all.at[frm, s], kv_all.at[frm, s], fkv_ss.at[d - 1, s], fkv_rs.at[d - 1, s],
                device_id=holder(me, frm), device_id_type=MESH).wait_recv()
            place_kv(frm, s)

    factor = LOG2E * size ** (-0.5)

    @pl.loop(0, HEADS // GROUP)
    def _(g):
        for n in range(GROUP):
            s = source_at(g * GROUP + n)

            @pl.when(s != me)
            def _():
                pltpu.make_async_remote_copy(
                    q_out.at[s], q_in.at[s], q_ss.at[s], q_rs.at[s],
                    device_id=holder(s, part), device_id_type=MESH).wait_recv()

            placed = jnp.dot(
                spread(part, s).astype(jnp.bfloat16), q_in[s], preferred_element_type=jnp.float32
            ).astype(jnp.bfloat16)
            for c in range(groups):
                q_slots[c, n * cap:(n + 1) * cap, :size] = placed[c * cap:(c + 1) * cap]

        @pl.loop(0, groups)
        def _(c):
            scores = lax.dot_general(
                q_slots[c], k_slots[c], (((1,), (1,)), ((), ())), preferred_element_type=jnp.float32
            )
            top = jnp.max(scores, axis=1, keepdims=True)
            weights = jnp.exp2((scores - top) * factor)
            total = jnp.sum(weights, axis=1, keepdims=True)
            summed = jnp.dot(
                weights.astype(jnp.bfloat16), v_slots[c], preferred_element_type=jnp.float32
            )
            att_slots[c] = (summed / total).astype(jnp.bfloat16)

        for n in range(GROUP):
            s = source_at(g * GROUP + n)
            mine = jnp.concatenate(
                [att_slots[c, n * cap:(n + 1) * cap, :] for c in range(groups)], axis=0
            )
            back = lax.dot_general(
                spread(part, s).astype(jnp.bfloat16), mine, (((0,), (0,)), ((), ())),
                preferred_element_type=jnp.float32,
            ).astype(jnp.bfloat16)
            ret_out[s] = back

            @pl.when(s != me)
            def _():
                ret_copy(s).start()

            @pl.when(s == me)
            def _():
                own = pltpu.make_async_copy(
                    ret_out.at[s], gathered.at[:, pl.ds(pl.multiple_of(me * size, size), size)], own_sem)
                own.start()
                own.wait()

    @pl.loop(0, HEADS)
    def _(h):
        @pl.when(h != me)
        def _():
            id_copy(h).wait_send()
            kv_copy(h).wait_send()
            q_copy(h).wait_send()
            ret_copy(h).wait_send()
            pltpu.make_async_remote_copy(
                ret_out.at[h], gathered.at[:, pl.ds(pl.multiple_of(h * size, size), size)],
                ret_ss.at[h], ret_rs.at[h], device_id=holder(h, part), device_id_type=MESH).wait_recv()

        for d in range(1, parts):
            id_fwd(h, d).wait_send()
            kv_fwd(h, d).wait_send()

    out_ref[...] = gathered[...]


def per_device(tokens, w_query, w_key, w_value, cluster_ids):
    groups, blks = lax.axis_size("cluster"), lax.axis_size("blk")
    rows, width = tokens.shape
    size = width // HEADS
    parts = groups * blks // HEADS
    cap = 4 * rows // (3 * groups)
    padded = -(-rows // 128) * 128
    lab_row = jnp.pad(cluster_ids.reshape(1, rows), ((0, 0), (0, padded - rows)), constant_values=-1)
    vmem = pl.BlockSpec(memory_space=pltpu.VMEM)
    hbm = pl.BlockSpec(memory_space=pl.ANY)
    bf16 = jnp.bfloat16
    sem = pltpu.SemaphoreType.DMA
    others = max(parts - 1, 1)
    keys = parts * HEADS * cap
    return pl.pallas_call(
        functools.partial(kernel, groups, blks, parts, cap),
        out_shape=jax.ShapeDtypeStruct((rows, width), bf16),
        in_specs=[vmem, hbm, hbm, hbm, vmem, vmem],
        out_specs=vmem,
        scratch_shapes=[
            pltpu.VMEM((2, width, 3 * PAIR * size), bf16),
            pltpu.VMEM((HEADS, rows, 2 * size), bf16),
            pltpu.VMEM((HEADS, rows, size), bf16),
            pltpu.VMEM((1, padded), jnp.int32),
            pltpu.VMEM((parts, HEADS, rows, 2 * size), bf16),
            pltpu.VMEM((HEADS, rows, size), bf16),
            pltpu.VMEM((parts, HEADS, 1, padded), jnp.int32),
            pltpu.VMEM((groups, keys, 2 * size), bf16),
            pltpu.VMEM((groups, keys, size), bf16),
            pltpu.VMEM((groups, GROUP * cap, 2 * size), bf16),
            pltpu.VMEM((groups, GROUP * cap, size), bf16),
            pltpu.VMEM((HEADS, rows, size), bf16),
            pltpu.VMEM((rows, width), bf16),
            sem((2, 3)),
            sem((HEADS,)), sem((HEADS,)), sem((HEADS,)), sem((HEADS,)), sem((HEADS,)), sem((HEADS,)),
            sem((others, HEADS)), sem((others, HEADS)), sem((others, HEADS)), sem((others, HEADS)),
            sem((HEADS,)), sem((HEADS,)),
            sem,
        ],
        compiler_params=pltpu.CompilerParams(
            collective_id=0, has_side_effects=True, vmem_limit_bytes=60 * 1024 * 1024
        ),
    )(tokens, w_query, w_key, w_value, lab_row, cluster_ids)


def solution(mesh):
    return jax.shard_map(
        per_device,
        mesh=mesh,
        in_specs=(P(("cluster", "blk"), None), P(), P(), P(), P(("cluster", "blk"), None)),
        out_specs=P(("cluster", "blk"), None),
        check_vma=False,
    )
```

time: 470 us -> 98.4 us (0.21)
  waiting for transfers between devices: 229 us -> 0 us
  Pallas kernels: 0 us -> 93.4 us
  matrix products: 79 us -> 0 us
  blocking collectives: 63.2 us -> 0 us
  local copies, waits for them, and re-layouts: 56.9 us -> 4.79 us
  other arithmetic: 21.2 us -> 0 us
  between operations: 13.5 us -> 0.01 us
  starting transfers between devices: 6.78 us -> 0 us
    all_gather x2 -> x0, waiting for transfers between devices: 210 us -> none  [the longest x1 115 us: per_device(): value_piece = lax.all_gather(v_rows, 'blk', axis=0, tiled=True)]
    pallas_call x0 -> x1, Pallas kernels: none -> 93.4 us  [per_device(): pl.pallas_call(functools.partial(kernel, groups, blks, parts, cap), out_s...]
    dot_general x19 -> x0, matrix products: 79 us -> none  [the longest x8 47.5 us: advance(): jnp.einsum('hqk,khd->qhd', softmax_w.astype(jnp.bfloat16), value_block, p...]
    all_to_all x1 -> x0, blocking collectives: 41.2 us -> none  [per_device(): lax.all_to_all(outgoing.reshape(groups, capacity, 3 * model_width), 'clus...]
    dynamic_slice x16 -> x0, local copies, waits for them, and re-layouts: 28 us -> none  [per_device(): lax.scan(advance, running, (key_blocks, value_blocks, live_blocks))]
    all_gather x1 -> x0, blocking collectives: 21.9 us -> none  [per_device(): live_piece = lax.all_gather(live_rows, 'blk', axis=0, tiled=True)]
    unnamed x16 -> x2, local copies, waits for them, and re-layouts: 22 us -> 3.53 us
    all_to_all x2 -> x0, waiting for transfers between devices: 18 us -> none  [the longest x1 14.4 us: per_device(): lax.all_to_all(attended.reshape(groups, capacity, model_width), 'cluster'...]
  transfers between devices with their start and end apart: 4 -> 0, of which waited for: 4 -> 0; matrix products, arithmetic and copies ran while one was open for 3% -> 0% of each run, Pallas kernels for 0% -> 0%
where the time goes in v1:
time: 98.4 us; the launch traced here: 98.2 us
  Pallas kernels  93.4 us (95%)
  local copies, waits for them, and re-layouts  4.79 us (5%)
    pallas_call x1, Pallas kernels, per_device(): pl.pallas_call(functools.partial(kernel, groups, blks, parts, cap), out_s...  93.4 us
    unnamed x2, local copies, waits for them, and re-layouts  3.53 us

profile of v1, /device:TPU:0, one launch (start us, length us, event | category | flops | bytes accessed | tf_op | source)
XLA Modules:
  0.0 98.2 jit_solution(4266806576178790405)
XLA Ops:
  0.0 1.3 %pad.4.lrow_ref = s32[1,256]{1,0:T(1,128)} pad(s32[1,192]{1,0:T(1,128)} %bitcast.1, s32[]{:T(128)} %constant.0.clone.1), padding=0_0x0_64 | pad | bytes 1796 | tf_op jit(solution)/shard_map/jit(_pad)/pad | solution.py:285
  1.3 1.4 %copy.6.lcol_ref = s32[192,1]{1,0:T(8,128)} copy(s32[192,1]{0,1:T(1,128)} %param.9) | data formatting | bytes 1536 | tf_op args[4]
  2.7 93.4 %shard_map.55 = bf16[192,2048]{1,0:T(8,128)(2,1)} custom-call(bf16[192,2048]{1,0:T(8,128)(2,1)} %tok_ref.1, bf16[2048,2048]{1,0:T(8,128)(2,1)} %wq_ref.1, bf16[2048,2048]{1,0:T(8,128)(2,1)} %wk_ref.1, bf16[2048,2048]{1,0:T(8,128)(2,1)} %wv_ref.1, s32[1,256]{1,0:T(1,128)} %pad.4.lrow_ref, s32[192,1]{1,0:T(8,128)} %copy.6.lcol_ref), custom_call_target="tpu_custom_call" | custom-call | tf_op jit(solution)/shard_map/pallas_call | solution.py:292
  96.1 2.1 %copy.8 = bf16[192,2048]{1,0:T(8,128)(2,1)} copy(bf16[192,2048]{1,0:T(8,128)(2,1)} %shard_map.55) | data formatting | bytes 1572864

commit v2 on v1

--- a/solution.py
+++ b/solution.py
@@ -15,7 +15,7 @@
 MESH = pl.DeviceIdType.MESH
 
 
-def kernel(groups, blks, parts, cap, tok_ref, wq_ref, wk_ref, wv_ref, lrow_ref, lcol_ref, out_ref,
+def kernel(groups, blks, parts, cap, tok_ref, wq_ref, wk_ref, wv_ref, lcol_ref, out_ref,
            w_buf, kv_out, q_out, ids_out, kv_all, q_in, ids_all, k_slots, v_slots, q_slots, att_slots,
            ret_out, gathered, w_sem, kv_ss, kv_rs, q_ss, q_rs, id_ss, id_rs, fkv_ss, fkv_rs, fid_ss,
            fid_rs, ret_ss, ret_rs, own_sem):
@@ -61,12 +61,11 @@
             barrier, inc=1, device_id=holder(me, lax.rem(part + d, parts)), device_id_type=MESH
         )
 
-    lab = lrow_ref[...]
-    padded = lab.shape[1]
-    earlier = (lcol_ref[...] == lab) & (
-        lax.broadcasted_iota(jnp.int32, (rows, padded), 0)
-        < lax.broadcasted_iota(jnp.int32, (rows, padded), 1)
-    )
+    padded = ids_out.shape[1]
+    above = lax.broadcasted_iota(jnp.int32, (rows, padded), 0)
+    across = lax.broadcasted_iota(jnp.int32, (rows, padded), 1)
+    lab = jnp.sum(jnp.where(above == across, lcol_ref[...] + 1, 0), axis=0, keepdims=True) - 1
+    earlier = (lcol_ref[...] == lab) & (above < across)
     rank = jnp.sum(earlier.astype(jnp.int32), axis=0, keepdims=True)
     target = jnp.where(lab >= 0, lab * cap + rank, -1)
     ids_out[...] = target
@@ -221,8 +220,7 @@
             for c in range(groups):
                 q_slots[c, n * cap:(n + 1) * cap, :size] = placed[c * cap:(c + 1) * cap]
 
-        @pl.loop(0, groups)
-        def _(c):
+        def attend(c):
             scores = lax.dot_general(
                 q_slots[c], k_slots[c], (((1,), (1,)), ((), ())), preferred_element_type=jnp.float32
             )
@@ -234,6 +232,12 @@
             )
             att_slots[c] = (summed / total).astype(jnp.bfloat16)
 
+        if groups <= 4:
+            for c in range(groups):
+                attend(c)
+        else:
+            pl.loop(0, groups)(attend)
+
         for n in range(GROUP):
             s = source_at(g * GROUP + n)
             mine = jnp.concatenate(
@@ -282,7 +286,6 @@
     parts = groups * blks // HEADS
     cap = 4 * rows // (3 * groups)
     padded = -(-rows // 128) * 128
-    lab_row = jnp.pad(cluster_ids.reshape(1, rows), ((0, 0), (0, padded - rows)), constant_values=-1)
     vmem = pl.BlockSpec(memory_space=pltpu.VMEM)
     hbm = pl.BlockSpec(memory_space=pl.ANY)
     bf16 = jnp.bfloat16
@@ -292,7 +295,7 @@
     return pl.pallas_call(
         functools.partial(kernel, groups, blks, parts, cap),
         out_shape=jax.ShapeDtypeStruct((rows, width), bf16),
-        in_specs=[vmem, hbm, hbm, hbm, vmem, vmem],
+        in_specs=[vmem, hbm, hbm, hbm, vmem],
         out_specs=vmem,
         scratch_shapes=[
             pltpu.VMEM((2, width, 3 * PAIR * size), bf16),
@@ -317,7 +320,7 @@
         compiler_params=pltpu.CompilerParams(
             collective_id=0, has_side_effects=True, vmem_limit_bytes=60 * 1024 * 1024
         ),
-    )(tokens, w_query, w_key, w_value, lab_row, cluster_ids)
+    )(tokens, w_query, w_key, w_value, cluster_ids)
 
 
 def solution(mesh):

time: 98.4 us -> 91.8 us (0.933)
  Pallas kernels: 93.4 us -> 88.1 us
  local copies, waits for them, and re-layouts: 4.79 us -> 3.53 us
    pallas_call x1, Pallas kernels: 93.4 us -> 88.1 us  [per_device(): pl.pallas_call(functools.partial(kernel, groups, blks, parts, cap), out_s...]
    pad x1 -> x0, local copies, waits for them, and re-layouts: 1.26 us -> none  [per_device(): jnp.pad(cluster_ids.reshape(1, rows), ((0, 0), (0, padded - rows)), const...]
where the time goes in v2:
time: 91.8 us; the launch traced here: 91.6 us
  Pallas kernels  88.1 us (96%)
  local copies, waits for them, and re-layouts  3.53 us (4%)
    pallas_call x1, Pallas kernels, per_device(): pl.pallas_call(functools.partial(kernel, groups, blks, parts, cap), out_s...  88.1 us
    unnamed x2, local copies, waits for them, and re-layouts  3.53 us

profile of v2, /device:TPU:0, one launch (start us, length us, event | category | flops | bytes accessed | tf_op | source)
XLA Modules:
  0.0 91.6 jit_solution(8200398037557440776)
XLA Ops:
  0.0 1.4 %copy.6.lcol_ref = s32[192,1]{1,0:T(8,128)} copy(s32[192,1]{0,1:T(1,128)} %param.9) | data formatting | bytes 1536 | tf_op args[4]
  1.4 88.1 %shard_map.55 = bf16[192,2048]{1,0:T(8,128)(2,1)} custom-call(bf16[192,2048]{1,0:T(8,128)(2,1)} %tok_ref.1, bf16[2048,2048]{1,0:T(8,128)(2,1)} %wq_ref.1, bf16[2048,2048]{1,0:T(8,128)(2,1)} %wk_ref.1, bf16[2048,2048]{1,0:T(8,128)(2,1)} %wv_ref.1, s32[192,1]{1,0:T(8,128)} %copy.6.lcol_ref), custom_call_target="tpu_custom_call" | custom-call | tf_op jit(solution)/shard_map/pallas_call | solution.py:295
  89.5 2.1 %copy.8 = bf16[192,2048]{1,0:T(8,128)(2,1)} copy(bf16[192,2048]{1,0:T(8,128)(2,1)} %shard_map.55) | data formatting | bytes 1572864

commit v3 on v2

--- a/solution.py
+++ b/solution.py
@@ -45,8 +45,9 @@
             for n, ref in enumerate((wq_ref, wk_ref, wv_ref))
         ]
 
-    for copy in w_copies(0, 0):
-        copy.start()
+    for t in range(2):
+        for copy in w_copies(t, t):
+            copy.start()
 
     barrier = pltpu.get_barrier_semaphore()
 
@@ -114,11 +115,11 @@
 
     @pl.loop(0, pairs)
     def _(t):
-        slot = lax.rem(t, 2)
-
-        @pl.when(t + 1 < pairs)
-        def _():
-            for copy in w_copies(t + 1, 1 - slot):
+        slot = lax.rem(t, 3)
+
+        @pl.when(t + 2 < pairs)
+        def _():
+            for copy in w_copies(t + 2, lax.rem(t + 2, 3)):
                 copy.start()
 
         for copy in w_copies(t, slot):
@@ -298,7 +299,7 @@
         in_specs=[vmem, hbm, hbm, hbm, vmem],
         out_specs=vmem,
         scratch_shapes=[
-            pltpu.VMEM((2, width, 3 * PAIR * size), bf16),
+            pltpu.VMEM((3, width, 3 * PAIR * size), bf16),
             pltpu.VMEM((HEADS, rows, 2 * size), bf16),
             pltpu.VMEM((HEADS, rows, size), bf16),
             pltpu.VMEM((1, padded), jnp.int32),
@@ -311,14 +312,14 @@
             pltpu.VMEM((groups, GROUP * cap, size), bf16),
             pltpu.VMEM((HEADS, rows, size), bf16),
             pltpu.VMEM((rows, width), bf16),
-            sem((2, 3)),
+            sem((3, 3)),
             sem((HEADS,)), sem((HEADS,)), sem((HEADS,)), sem((HEADS,)), sem((HEADS,)), sem((HEADS,)),
             sem((others, HEADS)), sem((others, HEADS)), sem((others, HEADS)), sem((others, HEADS)),
             sem((HEADS,)), sem((HEADS,)),
             sem,
         ],
         compiler_params=pltpu.CompilerParams(
-            collective_id=0, has_side_effects=True, vmem_limit_bytes=60 * 1024 * 1024
+            collective_id=0, has_side_effects=True, vmem_limit_bytes=62 * 1024 * 1024
         ),
     )(tokens, w_query, w_key, w_value, cluster_ids)
 

time: 91.8 us -> 90.7 us (0.988)
  Pallas kernels: 88.1 us -> 87 us
    pallas_call x1, Pallas kernels: 88.1 us -> 87 us  [per_device(): pl.pallas_call(functools.partial(kernel, groups, blks, parts, cap), out_s...]
where the time goes in v3:
time: 90.7 us; the launch traced here: 90.5 us
  Pallas kernels  87 us (96%)
  local copies, waits for them, and re-layouts  3.53 us (4%)
    pallas_call x1, Pallas kernels, per_device(): pl.pallas_call(functools.partial(kernel, groups, blks, parts, cap), out_s...  87 us
    unnamed x2, local copies, waits for them, and re-layouts  3.53 us

profile of v3, /device:TPU:0, one launch (start us, length us, event | category | flops | bytes accessed | tf_op | source)
XLA Modules:
  0.0 90.5 jit_solution(16354059827836085129)
XLA Ops:
  0.0 1.4 %copy.6.lcol_ref = s32[192,1]{1,0:T(8,128)} copy(s32[192,1]{0,1:T(1,128)} %param.9) | data formatting | bytes 1536 | tf_op args[4]
  1.4 87.0 %shard_map.55 = bf16[192,2048]{1,0:T(8,128)(2,1)} custom-call(bf16[192,2048]{1,0:T(8,128)(2,1)} %tok_ref.1, bf16[2048,2048]{1,0:T(8,128)(2,1)} %wq_ref.1, bf16[2048,2048]{1,0:T(8,128)(2,1)} %wk_ref.1, bf16[2048,2048]{1,0:T(8,128)(2,1)} %wv_ref.1, s32[192,1]{1,0:T(8,128)} %copy.6.lcol_ref), custom_call_target="tpu_custom_call" | custom-call | tf_op jit(solution)/shard_map/pallas_call | solution.py:296
  88.4 2.1 %copy.8 = bf16[192,2048]{1,0:T(8,128)(2,1)} copy(bf16[192,2048]{1,0:T(8,128)(2,1)} %shard_map.55) | data formatting | bytes 1572864
